TPU v7x, 32 devices: a whole 2x2x4 slice. The times are simulated.
32 devices in a mesh: gx: 4 (over y, x), gy: 8 (over z, core).
Axes of the slice: x: 2, y: 2, z: 4, core: 2. Of those that a mesh axis runs over, the one named last changes fastest.
Arguments:
- weights: float32 [4, 8, 64, 32, 128], P('gx', 'gy'), may hold values from -6 to 6
- coef_first: float32 [8, 6, 64], P('gy'), may hold values from 0.25 to 1
- coef_second: float32 [14, 64], replicated, may hold values from 0.25 to 1
Outputs:
- final_weights: float32 [8, 256, 32, 128], P('gy', 'gx')
All inputs are finite; a program needn't handle non-finite values.
Results may differ from a plain program's by a relative error of at most 0.0003.
Values sent between devices are 32-bit elements; how exact they have to be, the bound alone decides.
A program may use at most 64 MiB of HBM per device.

v0:
```python
import math

import jax
import jax.numpy as jnp
import numpy as np
from jax import lax
from jax.sharding import PartitionSpec as P

N = 4096
MX = 64
MY = 32


TWO_PI = 2.0 * math.pi


def from_partner(value, axis, apart):
    mask = 2**apart
    pairs = [(source, source ^ mask) for source in range(lax.axis_size(axis))]
    return lax.ppermute(value, axis, pairs)


def cheb_nodes():
    return np.cos(np.pi * (2.0 * np.arange(8) + 1.0) / 16.0)


def lagrange_child(child_half):
    nodes = cheb_nodes()
    targets = (2.0 * child_half - 1.0) / 2.0 + nodes / 2.0
    result = np.ones((8, 8))
    for target in range(8):
        for factor in range(8):
            if factor != target:
                result[target, :] = (
                    result[target, :] * (targets - nodes[factor]) / (nodes[target] - nodes[factor])
                )
    return result


def kron_stack(along_second):
    matrices = []
    for child_half in range(2):
        lagrange = lagrange_child(child_half)
        if along_second:
            middle = np.kron(np.eye(8), lagrange)
        else:
            middle = np.kron(lagrange, np.eye(8))
        matrices.append(np.kron(np.eye(2), middle).T)
    return jnp.asarray(np.stack(matrices), dtype=jnp.float32)


def node_pattern(along_second):
    nodes = cheb_nodes()
    if along_second:
        layout = np.tile(nodes, 8)
    else:
        layout = np.repeat(nodes, 8)
    return jnp.asarray(layout, dtype=jnp.float32)


def rotate_apply(values, phases, kernel):
    angles = phases * TWO_PI
    cosine = jnp.cos(angles)
    sines = jnp.sin(angles)
    real_part = values[..., :64]
    imag_part = values[..., 64:]
    rotated = jnp.concatenate(
        [cosine * real_part - sines * imag_part, sines * real_part + cosine * imag_part], axis=-1
    )
    mapped = jnp.dot(
        rotated.reshape(-1, 128),
        kernel,
        precision=lax.Precision.HIGHEST,
        preferred_element_type=jnp.float32,
    )
    return mapped.reshape(values.shape)


def bend_factor(centre, across, offset):
    shifted = centre - offset
    return (
        offset
        * (centre + shifted)
        / (
            jnp.sqrt(centre * centre + across * across)
            + jnp.sqrt(shifted * shifted + across * across)
        )
    )


def path_bits(device_pos, level_num):
    result = jnp.int32(0)
    for shift in range(level_num):
        result = result + ((device_pos >> shift & 1) << level_num - 1 - shift)
    return result


def x_term(current, table_rows, level_num, path_value, box_pos, pick_half, n_gx):
    freq_boxes = current.shape[0]
    columns = current.shape[1]
    box_width = N / (MX * 2**level_num)
    kernels = kron_stack(False)
    pattern = node_pattern(False)
    centre = (
        (jnp.arange(freq_boxes) * 2**level_num + path_value).astype(jnp.float32) + 0.5
    ) * box_width - N / 2
    across = (jnp.arange(columns).astype(jnp.float32) + 0.5) * (N / MY) - N / 2
    offset = box_width / 4 * (1 - 2 * pick_half).astype(jnp.float32)
    bending = bend_factor(centre[:, None], across[None, :], offset)
    location = (box_pos.astype(jnp.float32) + 0.5 + 0.5 * pattern) * (2**level_num / n_gx)
    start_row = sum((n_gx >> shift for shift in range(level_num)))
    coef_row = lax.dynamic_index_in_dim(table_rows, start_row + box_pos, 0, keepdims=False)
    phases = location[None, None, :] * offset + coef_row[None, None, :] * bending[:, :, None]
    return rotate_apply(current, phases, kernels[box_pos % 2])


def y_term(current, table_rows, level_num, path_value, box_pos, pick_half, n_gy, m_start, n_gx):
    row_count = current.shape[0]
    freq_boxes = current.shape[1]
    box_width = N / (MY * 2**level_num)
    kernels = kron_stack(True)
    pattern = node_pattern(True)
    leading = ((m_start + jnp.arange(row_count)).astype(jnp.float32) + 0.5) * (
        N / (MX * n_gx)
    ) - N / 2
    centre = (
        (jnp.arange(freq_boxes) * 2**level_num + path_value).astype(jnp.float32) + 0.5
    ) * box_width - N / 2
    offset = box_width / 4 * (1 - 2 * pick_half).astype(jnp.float32)
    bending = bend_factor(centre[None, :], leading[:, None], offset)
    location = (box_pos.astype(jnp.float32) + 0.5 + 0.5 * pattern) * (2**level_num / n_gy)
    start_row = sum((n_gy >> shift for shift in range(level_num)))
    coef_row = lax.dynamic_index_in_dim(table_rows, start_row + box_pos, 0, keepdims=False)
    phases = location[None, None, :] * offset + coef_row[None, None, :] * bending[:, :, None]
    return rotate_apply(current, phases, kernels[box_pos % 2])


def on_device(weights, coef_first, coef_second):
    n_gx = lax.axis_size("gx")
    n_gy = lax.axis_size("gy")
    x_bits = n_gx.bit_length() - 1
    y_bits = n_gy.bit_length() - 1
    gx_index = lax.axis_index("gx")
    gy_index = lax.axis_index("gy")
    table_first = coef_first[0]
    current = weights[0, 0]
    per_block = MX // n_gx
    for level_num in range(x_bits):
        box_pos = gx_index >> level_num
        own_half = box_pos % 2
        path_value = path_bits(gx_index, level_num)
        partner = from_partner(current, "gx", level_num)
        current = x_term(
            current, table_first, level_num, path_value, box_pos, own_half, n_gx
        ) + x_term(partner, table_first, level_num, path_value, box_pos ^ 1, own_half, n_gx)
    blocks = current.reshape(n_gx, per_block, MY, 128)
    gathered = lax.all_to_all(blocks, "gx", split_axis=0, concat_axis=0, tiled=True)
    gathered = gathered.reshape((2,) * x_bits + (per_block, MY, 128))
    gathered = jnp.transpose(
        gathered, tuple(reversed(range(x_bits))) + tuple(range(x_bits, x_bits + 3))
    )
    gathered = gathered.reshape(n_gx, per_block, MY, 128)
    current = jnp.transpose(gathered, (1, 0, 2, 3)).reshape(MX, MY, 128)
    m_start = gx_index * MX
    for level_num in range(y_bits):
        box_pos = gy_index >> level_num
        own_half = box_pos % 2
        path_value = path_bits(gy_index, level_num)
        partner = from_partner(current, "gy", level_num)
        current = y_term(
            current, coef_second, level_num, path_value, box_pos, own_half, n_gy, m_start, n_gx
        ) + y_term(
            partner, coef_second, level_num, path_value, box_pos ^ 1, own_half, n_gy, m_start, n_gx
        )
    return current[None]


def solution(mesh):
    in_specs = (P("gx", "gy", None, None, None), P("gy", None, None), P())
    out_specs = P("gy", "gx", None, None)
    return jax.shard_map(
        on_device, mesh=mesh, in_specs=in_specs, out_specs=out_specs, check_vma=False
    )
```

profile of v0, /device:TPU:0, one launch (start us, length us, event | category | flops | bytes accessed | tf_op | source)
XLA Modules:
  0.0 197.4 jit_solution(9677533101751282634)
XLA Ops:
  0.0 2.9 %collective-permute-start = (f32[64,32,128]{2,1,0:T(8,128)}, f32[64,32,128]{2,1,0:T(8,128)S(1)}, u32[]{:S(2)}, u32[]{:S(2)}) collective-permute-start(f32[64,32,128]{2,1,0:T(8,128)} %bitcast.74), channel_id=1, source_target_pairs={{0,8},{8,0},{16,24},{24,16},{1,9},{9,1},{17,25},{25,17},{2,10},{10... | collective-permute-start | bytes 3145736 | tf_op jit(solution)/shard_map/ppermute | solution.py:20
  3.2 0.1 add_divide_fusion.4
  3.3 0.1 copy.29
  3.4 0.7 copy-done.2
  4.1 0.6 copy-done.4
  4.7 21.6 %collective-permute-done = f32[64,32,128]{2,1,0:T(8,128)S(1)} collective-permute-done((f32[64,32,128]{2,1,0:T(8,128)}, f32[64,32,128]{2,1,0:T(8,128)S(1)}, u32[]{:S(2)}, u32[]{:S(2)}) %collective-permute-start) | collective-permute-done | bytes 1048608 | tf_op jit(solution)/shard_map/ppermute | solution.py:20
  26.3 9.8 %multiply_subtract_fusion.8 = (f32[64,32,64]{2,1,0:T(8,128)S(1)}, f32[64,32,64]{2,1,0:T(8,128)S(1)}, f32[64,32,64]{2,1,0:T(8,128)S(1)}, f32[64,32,64]{2,1,0:T(8,128)S(1)}) fusion(f32[64,32,128]{2,1,0:T(8,128)S(1)} %collective-permute-done, f32[64]{0:T(128)S(1)} %get-tuple-element.44, f32[64]{0:T(128)S(1)} %get-tuple-element.57, f32[64,32]{1,0:T(8,128)S(1)} %copy.29, ...), kind=kLoop, calls=%fused_computation.70 | loop fusion | flops 2359296 | bytes 4203520 | tf_op jit(solution)/shard_map/sub | solution.py:68
  36.2 1.0 fusion.1
  37.2 1.0 convolution_add_fusion.4
  38.3 1.8 collective-permute-start.1
  40.2 22.5 %collective-permute-done.1 = f32[64,32,128]{2,1,0:T(8,128)S(1)} collective-permute-done((f32[64,32,128]{2,1,0:T(8,128)S(1)}, f32[64,32,128]{2,1,0:T(8,128)S(1)}, u32[]{:S(2)}, u32[]{:S(2)}) %collective-permute-start.1) | collective-permute-done | bytes 1048608 | tf_op jit(solution)/shard_map/ppermute | solution.py:20
  62.7 8.4 %multiply_subtract_fusion.6 = (f32[64,32,64]{2,1,0:T(8,128)S(1)}, f32[64,32,64]{2,1,0:T(8,128)S(1)}, f32[64,32,64]{2,1,0:T(8,128)S(1)}, f32[64,32,64]{2,1,0:T(8,128)S(1)}) fusion(f32[64,32,128]{2,1,0:T(8,128)S(1)} %collective-permute-done.1, f32[64]{0:T(128)S(1)} %get-tuple-element.41, f32[64]{0:T(128)S(1)} %get-tuple-element.56, f32[64,32]{1,0:T(8,128)S(1)} %copy.28, ...), kind=kLoop, calls=%fused_computation.63 | loop fusion | flops 2359296 | bytes 4203520 | tf_op jit(solution)/shard_map/sub | solution.py:68
  71.1 1.0 fusion.8
  72.1 1.0 convolution_add_fusion.3
  73.2 15.8 %all_to_all.5 = f32[4,16,32,128]{3,2,1,0:T(8,128)S(1)} all-to-all(f32[4,16,32,128]{3,2,1,0:T(8,128)S(1)} %bitcast.76), channel_id=1, replica_groups=mesh['gx'=4,'gy'=8] {'gx'}, dimensions={0} | all-to-all | bytes 2097152 | tf_op jit(solution)/shard_map/all_to_all | solution.py:157
  89.0 0.1 copy.30
  89.2 0.1 copy.27
  89.3 0.9 fusion.100
  90.2 1.6 collective-permute-done.2
  91.8 8.4 %multiply_subtract_fusion.4 = (f32[64,32,64]{2,1,0:T(8,128)S(1)}, f32[64,32,64]{2,1,0:T(8,128)S(1)}, f32[64,32,64]{2,1,0:T(8,128)S(1)}, f32[64,32,64]{2,1,0:T(8,128)S(1)}) fusion(f32[64,32,128]{2,1,0:T(8,128)S(1)} %collective-permute-done.2, f32[64]{0:T(128)S(1)} %get-tuple-element.36, f32[64]{0:T(128)S(1)} %get-tuple-element.47, f32[64,32]{1,0:T(8,128)S(1)} %copy.27, ...), kind=kLoop, calls=%fused_computation.56 | loop fusion | flops 2359296 | bytes 4203520 | tf_op jit(solution)/shard_map/sub | solution.py:68
  100.2 1.0 fusion.15
  101.3 1.0 convolution_add_fusion.2
  102.3 1.6 collective-permute-start.3
  104.1 23.5 %collective-permute-done.3 = f32[64,32,128]{2,1,0:T(8,128)S(1)} collective-permute-done((f32[64,32,128]{2,1,0:T(8,128)S(1)}, f32[64,32,128]{2,1,0:T(8,128)S(1)}, u32[]{:S(2)}, u32[]{:S(2)}) %collective-permute-start.3) | collective-permute-done | bytes 1048608 | tf_op jit(solution)/shard_map/ppermute | solution.py:20
  127.6 8.4 %multiply_subtract_fusion.2 = (f32[64,32,64]{2,1,0:T(8,128)S(1)}, f32[64,32,64]{2,1,0:T(8,128)S(1)}, f32[64,32,64]{2,1,0:T(8,128)S(1)}, f32[64,32,64]{2,1,0:T(8,128)S(1)}) fusion(f32[64,32,128]{2,1,0:T(8,128)S(1)} %collective-permute-done.3, f32[64]{0:T(128)S(1)} %get-tuple-element.40, f32[64]{0:T(128)S(1)} %get-tuple-element.46, f32[64,32]{1,0:T(8,128)S(1)} %copy.26, ...), kind=kLoop, calls=%fused_computation.49 | loop fusion | flops 2359296 | bytes 4203520 | tf_op jit(solution)/shard_map/sub | solution.py:68
  136.0 1.0 fusion.22
  137.1 1.0 convolution_add_fusion.1
  138.1 2.7 %collective-permute-start.4 = (f32[64,32,128]{2,1,0:T(8,128)S(1)}, f32[64,32,128]{2,1,0:T(8,128)S(1)}, u32[]{:S(2)}, u32[]{:S(2)}) collective-permute-start(f32[64,32,128]{2,1,0:T(8,128)S(1)} %convolution_add_fusion.1), channel_id=1, source_target_pairs={{0,4},{1,5},{2,6},{3,7},{4,0},{5,1},{6,2},{7,3},{8,12},{9,13},{10,... | collective-permute-start | bytes 3145736 | tf_op jit(solution)/shard_map/ppermute | solution.py:20
  140.9 45.1 %collective-permute-done.4 = f32[64,32,128]{2,1,0:T(8,128)S(1)} collective-permute-done((f32[64,32,128]{2,1,0:T(8,128)S(1)}, f32[64,32,128]{2,1,0:T(8,128)S(1)}, u32[]{:S(2)}, u32[]{:S(2)}) %collective-permute-start.4) | collective-permute-done | bytes 1048608 | tf_op jit(solution)/shard_map/ppermute | solution.py:20
  185.9 8.4 %multiply_subtract_fusion = (f32[64,32,64]{2,1,0:T(8,128)S(1)}, f32[64,32,64]{2,1,0:T(8,128)S(1)}, f32[64,32,64]{2,1,0:T(8,128)S(1)}, f32[64,32,64]{2,1,0:T(8,128)S(1)}) fusion(f32[64,32,128]{2,1,0:T(8,128)S(1)} %collective-permute-done.4, f32[64]{0:T(128)S(1)} %get-tuple-element.35, f32[64]{0:T(128)S(1)} %get-tuple-element.45, f32[64,32]{1,0:T(8,128)S(1)} %copy.25, ...), kind=kLoop, calls=%fused_computation.42 | loop fusion | flops 2359296 | bytes 4203520 | tf_op jit(solution)/shard_map/sub | solution.py:68
  194.4 1.0 fusion.29
  195.4 2.0 %fusion = f32[1,64,32,128]{3,2,1,0:T(8,128)} fusion(f32[64,32,128]{2,1,0:T(8,128)S(1)} %fusion.29, f32[64,32,64]{2,1,0:T(8,128)S(1)} %get-tuple-element.6, f32[64,32,64]{2,1,0:T(8,128)S(1)} %get-tuple-element.5, f32[2,128,128]{2,1,0:T(8,128)S(1)} %copy-done, s32[]{:T(128)S(6)} %select_n.144), kind=kOutput, calls=%fused_computation.1 | convolution fusion | flops 403177472 | bytes 4259844 | tf_op jit(solution)/shard_map/dot_general | solution.py:70
  (24 shorter events, 0.4 us)
Async XLA Ops:
  0.0 26.3 %collective-permute-start = (f32[64,32,128]{2,1,0:T(8,128)}, f32[64,32,128]{2,1,0:T(8,128)S(1)}, u32[]{:S(2)}, u32[]{:S(2)}) collective-permute-start(f32[64,32,128]{2,1,0:T(8,128)} %bitcast.74), channel_id=1, source_target_pairs={{0,8},{8,0},{16,24},{24,16},{1,9},{9,1},{17,25},{25,17},{2,10},{10... | collective-permute-start | bytes 3145736 | tf_op jit(solution)/shard_map/ppermute | solution.py:20
  3.4 0.7 copy-start.2
  4.1 0.7 copy-start.4
  26.3 9.8 %copy-start.1 = (f32[2,128,128]{2,1,0:T(8,128)S(1)}, f32[2,128,128]{2,1,0:T(8,128)}, u32[]{:S(2)}) copy-start(f32[2,128,128]{2,1,0:T(8,128)} %constant.169.clone) | copy-start | bytes 393220
  38.3 24.4 %collective-permute-start.1 = (f32[64,32,128]{2,1,0:T(8,128)S(1)}, f32[64,32,128]{2,1,0:T(8,128)S(1)}, u32[]{:S(2)}, u32[]{:S(2)}) collective-permute-start(f32[64,32,128]{2,1,0:T(8,128)S(1)} %convolution_add_fusion.4), channel_id=1, source_target_pairs={{0,16},{8,24},{16,0},{24,8},{1,17},{9,25},{17,1},{25,9},{2,18},{10... | collective-permute-start | bytes 3145736 | tf_op jit(solution)/shard_map/ppermute | solution.py:20
  89.1 2.7 %collective-permute-start.2 = (f32[64,32,128]{2,1,0:T(8,128)S(1)}, f32[64,32,128]{2,1,0:T(8,128)S(1)}, u32[]{:S(2)}, u32[]{:S(2)}) collective-permute-start(f32[64,32,128]{2,1,0:T(8,128)S(1)} %bitcast.72), channel_id=1, source_target_pairs={{0,1},{1,0},{2,3},{3,2},{4,5},{5,4},{6,7},{7,6},{8,9},{9,8},{10,11... | collective-permute-start | bytes 3145736 | tf_op jit(solution)/shard_map/ppermute | solution.py:20
  89.3 0.9 copy-start.3
  91.8 8.4 %copy-start = (f32[2,128,128]{2,1,0:T(8,128)S(1)}, f32[2,128,128]{2,1,0:T(8,128)}, u32[]{:S(2)}) copy-start(f32[2,128,128]{2,1,0:T(8,128)} %constant.171.clone) | copy-start | bytes 393220
  102.3 25.3 %collective-permute-start.3 = (f32[64,32,128]{2,1,0:T(8,128)S(1)}, f32[64,32,128]{2,1,0:T(8,128)S(1)}, u32[]{:S(2)}, u32[]{:S(2)}) collective-permute-start(f32[64,32,128]{2,1,0:T(8,128)S(1)} %convolution_add_fusion.2), channel_id=1, source_target_pairs={{0,2},{1,3},{2,0},{3,1},{4,6},{5,7},{6,4},{7,5},{8,10},{9,11},{10,... | collective-permute-start | bytes 3145736 | tf_op jit(solution)/shard_map/ppermute | solution.py:20
  138.1 47.8 %collective-permute-start.4 = (f32[64,32,128]{2,1,0:T(8,128)S(1)}, f32[64,32,128]{2,1,0:T(8,128)S(1)}, u32[]{:S(2)}, u32[]{:S(2)}) collective-permute-start(f32[64,32,128]{2,1,0:T(8,128)S(1)} %convolution_add_fusion.1), channel_id=1, source_target_pairs={{0,4},{1,5},{2,6},{3,7},{4,0},{5,1},{6,2},{7,3},{8,12},{9,13},{10,... | collective-permute-start | bytes 3145736 | tf_op jit(solution)/shard_map/ppermute | solution.py:20
where the time goes:
time: 198 us; the launch traced here: 197 us
  waiting for transfers between devices  114 us (58%)
  other arithmetic  43.7 us (22%)
  blocking collectives  15.8 us (8%)
  matrix products  11.5 us (6%)
  starting transfers between devices  9.15 us (5%)
  local copies, waits for them, and re-layouts  2.68 us (1%)
    ppermute x5, waiting for transfers between devices, from_partner(): return lax.ppermute(value, axis, pairs)  114 us
    sub x5, other arithmetic, rotate_apply(): cosine * real_part - sines * imag_part  43.4 us
    all_to_all x1, blocking collectives, on_device(): lax.all_to_all(blocks, 'gx', split_axis=0, concat_axis=0, tiled=True)  15.8 us
    dot_general x10, matrix products, rotate_apply(): jnp.dot(rotated.reshape(-1, 128), kernel, precision=lax.Precision.HIGHEST...  11.5 us
    ppermute x5, starting transfers between devices, from_partner(): return lax.ppermute(value, axis, pairs)  9.15 us
  transfers between devices with their start and end apart: 5, of which 5 were waited for; matrix products, arithmetic and copies ran while one was open for 1% of the time, Pallas kernels for 0%

commit v1 on v0

--- a/solution.py
+++ b/solution.py
@@ -1,9 +1,12 @@
+import functools
 import math
 
 import jax
 import jax.numpy as jnp
 import numpy as np
 from jax import lax
+from jax.experimental import pallas as pl
+from jax.experimental.pallas import tpu as pltpu
 from jax.sharding import PartitionSpec as P
 
 N = 4096
@@ -175,9 +178,371 @@
     return current[None]
 
 
+LANES = 128
+MESH = pl.DeviceIdType.MESH
+
+
+def blocks_fit(n_gx, n_gy):
+    per_gx = MX // n_gx
+    if MX % n_gx or (per_gx * MY) % LANES or LANES % MY or n_gy % n_gx:
+        return False
+    return (per_gx * MY // LANES) % (n_gy // n_gx) == 0
+
+
+def chebyshev_fit(func, degree):
+    grid = 0.25 * (1 + np.cos(np.pi * (np.arange(400) + 0.5) / 400)) * 0.5
+    series = np.polynomial.chebyshev.Chebyshev.fit(grid, func(grid), degree, domain=[0.0, 0.25])
+    return [float(c) for c in series.convert(kind=np.polynomial.Polynomial).coef]
+
+
+def horner(coefs, arg):
+    result = coefs[-1]
+    for coef in coefs[-2::-1]:
+        result = result * arg + coef
+    return result
+
+
+COS_FIT = chebyshev_fit(lambda t: np.cos(np.pi * np.sqrt(t)), 5)
+SIN_FIT = chebyshev_fit(lambda t: 2.0 * np.sinc(np.sqrt(t)) * np.pi, 5)
+ROUNDER = 1.5 * 2.0**23
+
+
+def cos_sin_turns(turns):
+    part = turns - ((turns + ROUNDER) - ROUNDER)
+    square = part * part
+    cos_half = horner(COS_FIT, square)
+    twice_sin_half = horner(SIN_FIT, square) * part
+    return 1.0 - 0.5 * (twice_sin_half * twice_sin_half), twice_sin_half * cos_half
+
+
+def merge(load, coef, bending, scale, box, store):
+    nodes = cheb_nodes()
+    lagrange = lagrange_child(0)
+    plus = [[None] * 4, [None] * 4]
+    minus = [[None] * 4, [None] * 4]
+    bases = [scale * (2 * box + c + 0.5) for c in range(2)]
+    for s in range(8):
+        rotated = []
+        for c in range(2):
+            at = s if c == 0 else 7 - s
+            turns = coef(c, at) * bending + (bases[c] + scale * float(0.5 * nodes[at]))
+            cosine, sine = cos_sin_turns(turns)
+            real, imag = load(c, 0, at), load(c, 1, at)
+            rotated.append((cosine * real - sine * imag, sine * real + cosine * imag))
+        for r in range(2):
+            total = rotated[0][r] + rotated[1][r]
+            apart = rotated[0][r] - rotated[1][r]
+            for a in range(4):
+                even = total * float(0.5 * (lagrange[a, s] + lagrange[7 - a, s]))
+                odd = apart * float(0.5 * (lagrange[a, s] - lagrange[7 - a, s]))
+                plus[r][a] = even if s == 0 else plus[r][a] + even
+                minus[r][a] = odd if s == 0 else minus[r][a] + odd
+    for r in range(2):
+        for a in range(4):
+            store(r, a, plus[r][a] + minus[r][a])
+            store(r, 7 - a, plus[r][a] - minus[r][a])
+
+
+def wait_bytes(ref, sem):
+    pltpu.make_async_copy(ref, ref, sem).wait()
+
+
+def butterfly_kernel(
+    n_gx, n_gy, w_ref, cf_ref, cs_ref, o_ref,
+    x_in, x_a, x_b, x_out, y_in, y_a, y_b, y_t, y_out, cx, cy,
+    send_a, recv_a, send_b, recv_b, send_c, recv_c,
+):
+    gx = lax.axis_index("gx")
+    gy = lax.axis_index("gy")
+    x_bits = n_gx.bit_length() - 1
+    y_bits = n_gy.bit_length() - 1
+    per_gx = MX // n_gx
+    rows = LANES // MY
+    n_lb = per_gx // rows
+    fan = n_gy // n_gx
+    n_slot = n_lb // fan
+
+    barrier = pltpu.get_barrier_semaphore()
+    for step in range(1, n_gx):
+        pl.semaphore_signal(
+            barrier, inc=1, device_id=((gx + step) % n_gx, gy), device_id_type=MESH
+        )
+    for step in range(1, n_gy):
+        pl.semaphore_signal(
+            barrier, inc=1, device_id=(gx, (gy + step) % n_gy), device_id_type=MESH
+        )
+    pl.semaphore_wait(barrier, n_gx + n_gy - 2)
+
+    def first_copy(lb, step):
+        peer = (gx + step) % n_gx
+        return pltpu.make_async_remote_copy(
+            src_ref=w_ref.at[peer * n_lb + lb],
+            dst_ref=x_in.at[gx, lb],
+            send_sem=send_a.at[lb, step],
+            recv_sem=recv_a.at[lb, gx],
+            device_id=(peer, gy),
+            device_id_type=MESH,
+        )
+
+    for lb in range(n_lb):
+        for step in range(1, n_gx):
+            first_copy(lb, step).start()
+        pltpu.make_async_copy(
+            w_ref.at[gx * n_lb + lb], x_in.at[gx, lb], recv_a.at[lb, gx]
+        ).start()
+
+    for source, spread in ((cf_ref, cx), (cs_ref, cy)):
+        for row in range(source.shape[0]):
+            line = jnp.broadcast_to(source[row : row + 1, :], (LANES, 64))
+            spread[row] = line.T
+
+    lane = lax.broadcasted_iota(jnp.int32, (8, LANES), 1)
+    lane_m = lane // MY
+    lane_b = lane % MY
+    second = (lane_b.astype(jnp.float32) + 0.5) * (N / MY) - N / 2
+
+    def first_block(lb):
+        return gx * per_gx + lb * rows + lane_m
+
+    def second_peer(lb, step):
+        return (gy // fan + step) % n_gx * fan + lb % fan
+
+    def second_copy(lb, peer, gets_local):
+        z = peer // fan
+        slot = lb // fan
+        if gets_local:
+            return pltpu.make_async_copy(
+                x_out.at[lb, z], y_in.at[slot, gy], recv_b.at[slot, gy]
+            )
+        return pltpu.make_async_remote_copy(
+            src_ref=x_out.at[lb, z],
+            dst_ref=y_in.at[slot, gy],
+            send_sem=send_b.at[lb, z],
+            recv_sem=recv_b.at[slot, gy],
+            device_id=(gx, peer),
+            device_id_type=MESH,
+        )
+
+    def x_block(lb, carry):
+        for i in range(n_gx):
+            wait_bytes(x_in.at[i, lb], recv_a.at[lb, i])
+
+        def turn(i, carry):
+            x_a[i] = x_in[i, lb].T
+            return carry
+
+        lax.fori_loop(0, n_gx, turn, 0)
+        held, other = x_a, x_b
+        for level in range(x_bits):
+            halves = n_gx >> level + 1
+            width = N / (MX * 2**level)
+            start = sum(n_gx >> k for k in range(level))
+            last = level == x_bits - 1
+            target = x_out.at[lb] if last else other
+
+            def unit(u, carry, held=held, target=target, halves=halves, width=width,
+                     start=start, level=level):
+                box = u % halves
+                path = u // halves
+                sign = (1 - 2 * (path % 2)).astype(jnp.float32)
+                centre = (
+                    (first_block(lb) * 2**level + path // 2).astype(jnp.float32) + 0.5
+                ) * width - N / 2
+                bending = bend_factor(centre, second, sign * (width / 4))
+                at = path // 2 * (2 * halves) + 2 * box
+
+                def load(c, r, s):
+                    return held[at + c, r * 64 + s * 8 : r * 64 + s * 8 + 8, :]
+
+                def coef(c, s):
+                    return cx[start + 2 * box + c, s * 8 : s * 8 + 8, :]
+
+                def store(r, a, value):
+                    target[u, r * 64 + a * 8 : r * 64 + a * 8 + 8, :] = value
+
+                scale = sign * (width / 4 * 2**level / n_gx)
+                merge(load, coef, bending, scale, box.astype(jnp.float32), store)
+                return carry
+
+            lax.fori_loop(0, n_gx, unit, 0)
+            held, other = target, held
+
+        def send(step, carry):
+            peer = second_peer(lb, step + n_gx // 2)
+
+            @pl.when(peer == gy)
+            def _():
+                second_copy(lb, peer, True).start()
+
+            @pl.when(peer != gy)
+            def _():
+                second_copy(lb, peer, False).start()
+
+            return carry
+
+        lax.fori_loop(0, n_gx, send, 0)
+        return carry
+
+    lax.fori_loop(0, n_lb, x_block, 0)
+
+    def reverse(value):
+        result = 0
+        for shift in range(y_bits):
+            result = result * 2 + value // 2**shift % 2
+        return result
+
+    def third_copy(slot, peer, gets_local):
+        here = slot * fan + gy % fan
+        place = o_ref.at[here, :, gy // fan]
+        if gets_local:
+            return pltpu.make_async_copy(y_out.at[slot, peer], place, recv_c.at[slot, gy])
+        return pltpu.make_async_remote_copy(
+            src_ref=y_out.at[slot, peer],
+            dst_ref=place,
+            send_sem=send_c.at[slot, peer],
+            recv_sem=recv_c.at[slot, gy],
+            device_id=(gx, peer),
+            device_id_type=MESH,
+        )
+
+    def y_block(slot, carry):
+        lb = slot * fan + gy % fan
+        leading = (
+            (first_block(lb) * n_gx + gy // fan).astype(jnp.float32) + 0.5
+        ) * (N / (MX * n_gx)) - N / 2
+        for j in range(n_gy):
+            wait_bytes(y_in.at[slot, j], recv_b.at[slot, j])
+
+        held, target = y_in.at[slot], y_a
+        for level in range(y_bits):
+            halves = n_gy >> level + 1
+            width = N / (MY * 2**level)
+            start = sum(n_gy >> k for k in range(level))
+            last = level == y_bits - 1
+
+            def unit(t, carry, held=held, target=target, halves=halves, width=width,
+                     start=start, level=level, last=last):
+                if last:
+                    peer = (gy + n_gy // 2 + t) % n_gy
+                    u = reverse(peer)
+                else:
+                    u = t
+                box = u % halves
+                path = u // halves
+                sign = (1 - 2 * (path % 2)).astype(jnp.float32)
+                centre = (
+                    (lane_b * 2**level + path // 2).astype(jnp.float32) + 0.5
+                ) * width - N / 2
+                bending = bend_factor(centre, leading, sign * (width / 4))
+                at = path // 2 * (2 * halves) + 2 * box
+
+                def load(c, r, s):
+                    if level == 0:
+                        return held[at + c, pl.ds(r * 64 + s, 8, stride=8), :]
+                    return held[at + c, r * 64 + s * 8 : r * 64 + s * 8 + 8, :]
+
+                def coef(c, s):
+                    return cy[start + 2 * box + c, pl.ds(s, 8, stride=8), :]
+
+                def store(r, b, value):
+                    if last:
+                        y_t[pl.ds(r * 64 + b, 8, stride=8), :] = value
+                    else:
+                        target[u, r * 64 + b * 8 : r * 64 + b * 8 + 8, :] = value
+
+                scale = sign * (width / 4 * 2**level / n_gy)
+                merge(load, coef, bending, scale, box.astype(jnp.float32), store)
+                if last:
+                    y_out[slot, peer] = y_t[...].T.reshape(rows, MY, LANES)
+
+                    @pl.when(peer == gy)
+                    def _():
+                        third_copy(slot, peer, True).start()
+
+                    @pl.when(peer != gy)
+                    def _():
+                        third_copy(slot, peer, False).start()
+
+                return carry
+
+            lax.fori_loop(0, n_gy, unit, 0)
+            held, target = target, (y_b if target is y_a else y_a)
+        return carry
+
+    lax.fori_loop(0, n_slot, y_block, 0)
+
+    for lb in range(n_lb):
+        for step in range(1, n_gx):
+            first_copy(lb, step).wait_send()
+        for step in range(n_gx):
+            peer = second_peer(lb, step)
+
+            @pl.when(peer != gy)
+            def _():
+                second_copy(lb, peer, False).wait_send()
+
+    for slot in range(n_slot):
+        for step in range(1, n_gy):
+            third_copy(slot, (gy + step) % n_gy, False).wait_send()
+        for j in range(n_gy):
+            wait_bytes(o_ref.at[slot * fan + j % fan, :, j // fan], recv_c.at[slot, j])
+
+
+def by_blocks(weights, coef_first, coef_second):
+    n_gx = lax.axis_size("gx")
+    n_gy = lax.axis_size("gy")
+    per_gx = MX // n_gx
+    rows = LANES // MY
+    n_lb = per_gx // rows
+    n_slot = n_lb // (n_gy // n_gx)
+    block = (LANES, LANES)
+    vmem = functools.partial(pltpu.VMEM, dtype=jnp.float32)
+    dma = pltpu.SemaphoreType.DMA
+    table_first = coef_first[0]
+    finished = pl.pallas_call(
+        functools.partial(butterfly_kernel, n_gx, n_gy),
+        out_shape=jax.ShapeDtypeStruct((n_lb, rows, n_gx, MY, LANES), jnp.float32),
+        in_specs=[
+            pl.BlockSpec(memory_space=pl.ANY),
+            pl.BlockSpec(memory_space=pltpu.VMEM),
+            pl.BlockSpec(memory_space=pltpu.VMEM),
+        ],
+        out_specs=pl.BlockSpec(memory_space=pl.ANY),
+        scratch_shapes=[
+            vmem((n_gx, n_lb) + block),
+            vmem((n_gx,) + block),
+            vmem((n_gx,) + block),
+            vmem((n_lb, n_gx) + block),
+            vmem((n_slot, n_gy) + block),
+            vmem((n_gy,) + block),
+            vmem((n_gy,) + block),
+            vmem(block),
+            vmem((n_slot, n_gy, rows, MY, LANES)),
+            vmem((table_first.shape[0], 64, LANES)),
+            vmem((coef_second.shape[0], 64, LANES)),
+            dma((n_lb, n_gx)),
+            dma((n_lb, n_gx)),
+            dma((n_lb, n_gx)),
+            dma((n_slot, n_gy)),
+            dma((n_slot, n_gy)),
+            dma((n_slot, n_gy)),
+        ],
+        compiler_params=pltpu.CompilerParams(
+            collective_id=0, has_side_effects=True, vmem_limit_bytes=56 * 2**20
+        ),
+        name="butterfly",
+    )(weights.reshape(n_gx * n_lb, LANES, LANES), table_first, coef_second)
+    return finished.reshape(1, per_gx * n_gx, MY, LANES)
+
+
 def solution(mesh):
     in_specs = (P("gx", "gy", None, None, None), P("gy", None, None), P())
     out_specs = P("gy", "gx", None, None)
+    fits = blocks_fit(mesh.shape["gx"], mesh.shape["gy"])
     return jax.shard_map(
-        on_device, mesh=mesh, in_specs=in_specs, out_specs=out_specs, check_vma=False
+        by_blocks if fits else on_device,
+        mesh=mesh,
+        in_specs=in_specs,
+        out_specs=out_specs,
+        check_vma=False,
     )

time: 198 us -> 63.7 us (0.32)
  waiting for transfers between devices: 114 us -> 0 us
  Pallas kernels: 0 us -> 59.9 us
  other arithmetic: 43.7 us -> 0 us
  blocking collectives: 15.8 us -> 0 us
  matrix products: 11.5 us -> 0 us
  starting transfers between devices: 9.15 us -> 0 us
    ppermute x5 -> x0, waiting for transfers between devices: 114 us -> none  [from_partner(): return lax.ppermute(value, axis, pairs)]
    pallas_call x0 -> x1, Pallas kernels: none -> 59.9 us  [by_blocks(): pl.pallas_call(functools.partial(butterfly_kernel, n_gx, n_gy), out_shape...]
    sub x5 -> x0, other arithmetic: 43.4 us -> none  [rotate_apply(): cosine * real_part - sines * imag_part]
    all_to_all x1 -> x0, blocking collectives: 15.8 us -> none  [on_device(): lax.all_to_all(blocks, 'gx', split_axis=0, concat_axis=0, tiled=True)]
    dot_general x10 -> x0, matrix products: 11.5 us -> none  [rotate_apply(): jnp.dot(rotated.reshape(-1, 128), kernel, precision=lax.Precision.HIGHEST...]
    ppermute x5 -> x0, starting transfers between devices: 9.15 us -> none  [from_partner(): return lax.ppermute(value, axis, pairs)]
    unnamed x10 -> x2, local copies, waits for them, and re-layouts: 1.34 us -> 3.54 us
  transfers between devices with their start and end apart: 5 -> 0, of which waited for: 5 -> 0; matrix products, arithmetic and copies ran while one was open for 1% -> 0% of each run, Pallas kernels for 0% -> 0%
where the time goes in v1:
time: 63.7 us; the launch traced here: 63.4 us
  Pallas kernels  59.9 us (94%)
  local copies, waits for them, and re-layouts  3.54 us (6%)
    pallas_call x1, Pallas kernels, by_blocks(): pl.pallas_call(functools.partial(butterfly_kernel, n_gx, n_gy), out_shape...  59.9 us
    unnamed x2, local copies, waits for them, and re-layouts  3.54 us

profile of v1, /device:TPU:0, one launch (start us, length us, event | category | flops | bytes accessed | tf_op | source)
XLA Modules:
  0.0 63.4 jit_solution(9704108384344961766)
XLA Ops:
  0.0 1.3 %copy.6 = f32[1,6,64]{2,1,0:T(8,128)} copy(f32[1,6,64]{2,0,1:T(1,128)} %param.4) | data formatting | bytes 3072
  1.3 59.9 %butterfly.1 = f32[4,4,4,32,128]{4,3,2,1,0:T(8,128)} custom-call(f32[16,128,128]{2,1,0:T(8,128)} %bitcast.6, f32[6,64]{1,0:T(8,128)} %bitcast.7, f32[14,64]{1,0:T(8,128)} %cs_ref.1), custom_call_target="tpu_custom_call" | custom-call | tf_op jit(solution)/shard_map/butterfly/pallas_call | solution.py:502
  61.2 2.3 %copy.8 = f32[1,64,32,128]{3,2,1,0:T(8,128)} copy(f32[1,64,32,128]{3,2,1,0:T(8,128)} %bitcast.5) | data formatting | bytes 2097152

commit v2 on v1

--- a/solution.py
+++ b/solution.py
@@ -179,6 +179,8 @@
 
 
 LANES = 128
+AHEAD = 1
+HOLD = 0
 MESH = pl.DeviceIdType.MESH
 
 
@@ -284,16 +286,19 @@
             device_id_type=MESH,
         )
 
-    for lb in range(n_lb):
+    def first_start(lb):
         for step in range(1, n_gx):
             first_copy(lb, step).start()
         pltpu.make_async_copy(
             w_ref.at[gx * n_lb + lb], x_in.at[gx, lb], recv_a.at[lb, gx]
         ).start()
 
+    for lb in range(min(AHEAD, n_lb)):
+        first_start(lb)
+
     for source, spread in ((cf_ref, cx), (cs_ref, cy)):
         for row in range(source.shape[0]):
-            line = jnp.broadcast_to(source[row : row + 1, :], (LANES, 64))
+            line = jnp.broadcast_to(source[row].reshape(1, 64), (LANES, 64))
             spread[row] = line.T
 
     lane = lax.broadcasted_iota(jnp.int32, (8, LANES), 1)
@@ -327,6 +332,10 @@
         for i in range(n_gx):
             wait_bytes(x_in.at[i, lb], recv_a.at[lb, i])
 
+        @pl.when(lb + AHEAD < n_lb)
+        def _():
+            first_start(lb + AHEAD)
+
         def turn(i, carry):
             x_a[i] = x_in[i, lb].T
             return carry
@@ -405,6 +414,15 @@
             device_id_type=MESH,
         )
 
+    def third_start(slot, peer):
+        @pl.when(peer == gy)
+        def _():
+            third_copy(slot, peer, True).start()
+
+        @pl.when(peer != gy)
+        def _():
+            third_copy(slot, peer, False).start()
+
     def y_block(slot, carry):
         lb = slot * fan + gy % fan
         leading = (
@@ -412,6 +430,14 @@
         ) * (N / (MX * n_gx)) - N / 2
         for j in range(n_gy):
             wait_bytes(y_in.at[slot, j], recv_b.at[slot, j])
+
+        def held_back(t, carry):
+            third_start(slot - 1, (gy + n_gy // 2 + t) % n_gy)
+            return carry
+
+        @pl.when((slot >= 1) & (slot <= HOLD))
+        def _():
+            lax.fori_loop(0, n_gy, held_back, 0)
 
         held, target = y_in.at[slot], y_a
         for level in range(y_bits):
@@ -455,13 +481,9 @@
                 if last:
                     y_out[slot, peer] = y_t[...].T.reshape(rows, MY, LANES)
 
-                    @pl.when(peer == gy)
+                    @pl.when(slot >= HOLD)
                     def _():
-                        third_copy(slot, peer, True).start()
-
-                    @pl.when(peer != gy)
-                    def _():
-                        third_copy(slot, peer, False).start()
+                        third_start(slot, peer)
 
                 return carry
 
@@ -498,12 +520,12 @@
     block = (LANES, LANES)
     vmem = functools.partial(pltpu.VMEM, dtype=jnp.float32)
     dma = pltpu.SemaphoreType.DMA
-    table_first = coef_first[0]
+    table_first = jnp.transpose(coef_first, (1, 0, 2))
     finished = pl.pallas_call(
         functools.partial(butterfly_kernel, n_gx, n_gy),
         out_shape=jax.ShapeDtypeStruct((n_lb, rows, n_gx, MY, LANES), jnp.float32),
         in_specs=[
-            pl.BlockSpec(memory_space=pl.ANY),
+            pl.BlockSpec(memory_space=pltpu.HBM),
             pl.BlockSpec(memory_space=pltpu.VMEM),
             pl.BlockSpec(memory_space=pltpu.VMEM),
         ],
@@ -528,7 +550,7 @@
             dma((n_slot, n_gy)),
         ],
         compiler_params=pltpu.CompilerParams(
-            collective_id=0, has_side_effects=True, vmem_limit_bytes=56 * 2**20
+            collective_id=0, has_side_effects=True, vmem_limit_bytes=52 * 2**20
         ),
         name="butterfly",
     )(weights.reshape(n_gx * n_lb, LANES, LANES), table_first, coef_second)

time: 63.7 us -> 61.2 us (0.961)
  Pallas kernels: 59.9 us -> 58.6 us
  local copies, waits for them, and re-layouts: 3.54 us -> 2.35 us
    pallas_call x1, Pallas kernels: 59.9 us -> 58.6 us  [by_blocks(): pl.pallas_call(functools.partial(butterfly_kernel, n_gx, n_gy), out_shape...]
    unnamed x2 -> x5, local copies, waits for them, and re-layouts: 3.54 us -> 2.35 us
where the time goes in v2:
time: 61.2 us; the launch traced here: 61 us
  Pallas kernels  58.6 us (96%)
  local copies, waits for them, and re-layouts  2.35 us (4%)
    pallas_call x1, Pallas kernels, by_blocks(): pl.pallas_call(functools.partial(butterfly_kernel, n_gx, n_gy), out_shape...  58.6 us
    unnamed x5, local copies, waits for them, and re-layouts  2.35 us

profile of v2, /device:TPU:0, one launch (start us, length us, event | category | flops | bytes accessed | tf_op | source)
XLA Modules:
  0.0 61.0 jit_solution(14626034523680835727)
XLA Ops:
  0.0 0.0 copy-start.1
  0.0 0.7 %copy-done.1 = f32[1,6,64]{2,0,1:T(1,128)S(1)} copy-done((f32[1,6,64]{2,0,1:T(1,128)S(1)}, f32[1,6,64]{2,0,1:T(1,128)}, u32[]{:S(2)}) %copy-start.1) | copy-done | bytes 1560
  0.7 0.0 copy-start
  0.7 0.7 %copy-done = f32[14,64]{1,0:T(8,128)S(1)} copy-done((f32[14,64]{1,0:T(8,128)S(1)}, f32[14,64]{1,0:T(8,128)}, u32[]{:S(2)}) %copy-start) | copy-done | bytes 3608
  1.4 58.6 %butterfly.1 = f32[4,4,4,32,128]{4,3,2,1,0:T(8,128)S(1)} custom-call(f32[16,128,128]{2,1,0:T(8,128)} %bitcast.5, f32[6,1,64]{2,1,0:T(1,128)S(1)} %bitcast.4, f32[14,64]{1,0:T(8,128)S(1)} %copy-done), custom_call_target="tpu_custom_call" | custom-call | tf_op jit(solution)/shard_map/butterfly/pallas_call | solution.py:524
  60.0 1.0 %copy.5 = f32[1,64,32,128]{3,2,1,0:T(8,128)} copy(f32[1,64,32,128]{3,2,1,0:T(8,128)S(1)} %bitcast.3) | data formatting | bytes 2097152
Async XLA Ops:
  0.0 0.7 %copy-start.1 = (f32[1,6,64]{2,0,1:T(1,128)S(1)}, f32[1,6,64]{2,0,1:T(1,128)}, u32[]{:S(2)}) copy-start(f32[1,6,64]{2,0,1:T(1,128)} %param.4) | copy-start | bytes 4612
  0.7 0.7 %copy-start = (f32[14,64]{1,0:T(8,128)S(1)}, f32[14,64]{1,0:T(8,128)}, u32[]{:S(2)}) copy-start(f32[14,64]{1,0:T(8,128)} %cs_ref.1) | copy-start | bytes 10756

commit v3 on v2

--- a/solution.py
+++ b/solution.py
@@ -328,6 +328,15 @@
             device_id_type=MESH,
         )
 
+    def second_start(lb, peer):
+        @pl.when(peer == gy)
+        def _():
+            second_copy(lb, peer, True).start()
+
+        @pl.when(peer != gy)
+        def _():
+            second_copy(lb, peer, False).start()
+
     def x_block(lb, carry):
         for i in range(n_gx):
             wait_bytes(x_in.at[i, lb], recv_a.at[lb, i])
@@ -349,8 +358,9 @@
             last = level == x_bits - 1
             target = x_out.at[lb] if last else other
 
-            def unit(u, carry, held=held, target=target, halves=halves, width=width,
-                     start=start, level=level):
+            def unit(t, carry, held=held, target=target, halves=halves, width=width,
+                     start=start, level=level, last=last):
+                u = (gy // fan + n_gx // 2 + t) % n_gx if last else t
                 box = u % halves
                 path = u // halves
                 sign = (1 - 2 * (path % 2)).astype(jnp.float32)
@@ -371,25 +381,13 @@
 
                 scale = sign * (width / 4 * 2**level / n_gx)
                 merge(load, coef, bending, scale, box.astype(jnp.float32), store)
+                if last:
+                    second_start(lb, u * fan + lb % fan)
                 return carry
 
             lax.fori_loop(0, n_gx, unit, 0)
             held, other = target, held
 
-        def send(step, carry):
-            peer = second_peer(lb, step + n_gx // 2)
-
-            @pl.when(peer == gy)
-            def _():
-                second_copy(lb, peer, True).start()
-
-            @pl.when(peer != gy)
-            def _():
-                second_copy(lb, peer, False).start()
-
-            return carry
-
-        lax.fori_loop(0, n_gx, send, 0)
         return carry
 
     lax.fori_loop(0, n_lb, x_block, 0)

time: 61.2 us -> 60.8 us (level)
  no operation moved by 1% of the time
where the time goes in v3:
time: 60.8 us; the launch traced here: 60.6 us
  Pallas kernels  58.2 us (96%)
  local copies, waits for them, and re-layouts  2.35 us (4%)
    pallas_call x1, Pallas kernels, by_blocks(): pl.pallas_call(functools.partial(butterfly_kernel, n_gx, n_gy), out_shape...  58.2 us
    unnamed x5, local copies, waits for them, and re-layouts  2.35 us

profile of v3, /device:TPU:0, one launch (start us, length us, event | category | flops | bytes accessed | tf_op | source)
XLA Modules:
  0.0 60.6 jit_solution(4698852653749756168)
XLA Ops:
  0.0 0.0 copy-start.1
  0.0 0.7 %copy-done.1 = f32[1,6,64]{2,0,1:T(1,128)S(1)} copy-done((f32[1,6,64]{2,0,1:T(1,128)S(1)}, f32[1,6,64]{2,0,1:T(1,128)}, u32[]{:S(2)}) %copy-start.1) | copy-done | bytes 1560
  0.7 0.0 copy-start
  0.7 0.7 %copy-done = f32[14,64]{1,0:T(8,128)S(1)} copy-done((f32[14,64]{1,0:T(8,128)S(1)}, f32[14,64]{1,0:T(8,128)}, u32[]{:S(2)}) %copy-start) | copy-done | bytes 3608
  1.4 58.2 %butterfly.1 = f32[4,4,4,32,128]{4,3,2,1,0:T(8,128)S(1)} custom-call(f32[16,128,128]{2,1,0:T(8,128)} %bitcast.5, f32[6,1,64]{2,1,0:T(1,128)S(1)} %bitcast.4, f32[14,64]{1,0:T(8,128)S(1)} %copy-done), custom_call_target="tpu_custom_call" | custom-call | tf_op jit(solution)/shard_map/butterfly/pallas_call | solution.py:522
  59.6 1.0 %copy.5 = f32[1,64,32,128]{3,2,1,0:T(8,128)} copy(f32[1,64,32,128]{3,2,1,0:T(8,128)S(1)} %bitcast.3) | data formatting | bytes 2097152
Async XLA Ops:
  0.0 0.7 %copy-start.1 = (f32[1,6,64]{2,0,1:T(1,128)S(1)}, f32[1,6,64]{2,0,1:T(1,128)}, u32[]{:S(2)}) copy-start(f32[1,6,64]{2,0,1:T(1,128)} %param.4) | copy-start | bytes 4612
  0.7 0.7 %copy-start = (f32[14,64]{1,0:T(8,128)S(1)}, f32[14,64]{1,0:T(8,128)}, u32[]{:S(2)}) copy-start(f32[14,64]{1,0:T(8,128)} %cs_ref.1) | copy-start | bytes 10756

commit v4 on v3

--- a/solution.py
+++ b/solution.py
@@ -180,7 +180,7 @@
 
 LANES = 128
 AHEAD = 1
-HOLD = 0
+HOLD = 1
 MESH = pl.DeviceIdType.MESH
 
 
@@ -245,6 +245,12 @@
             store(r, 7 - a, plus[r][a] - minus[r][a])
 
 
+def far_first(me, count, step):
+    half = count // 2
+    side = (me // half + 1 + step // half) % 2
+    return side * half + (me % half + half // 2 + step) % half
+
+
 def wait_bytes(ref, sem):
     pltpu.make_async_copy(ref, ref, sem).wait()
 
@@ -360,7 +366,7 @@
 
             def unit(t, carry, held=held, target=target, halves=halves, width=width,
                      start=start, level=level, last=last):
-                u = (gy // fan + n_gx // 2 + t) % n_gx if last else t
+                u = far_first(gy // fan, n_gx, t) if last else t
                 box = u % halves
                 path = u // halves
                 sign = (1 - 2 * (path % 2)).astype(jnp.float32)
@@ -447,7 +453,7 @@
             def unit(t, carry, held=held, target=target, halves=halves, width=width,
                      start=start, level=level, last=last):
                 if last:
-                    peer = (gy + n_gy // 2 + t) % n_gy
+                    peer = far_first(gy, n_gy, t)
                     u = reverse(peer)
                 else:
                     u = t

time: 60.8 us -> 60 us (0.987)
  Pallas kernels: 58.2 us -> 57.3 us
    pallas_call x1, Pallas kernels: 58.2 us -> 57.3 us  [by_blocks(): pl.pallas_call(functools.partial(butterfly_kernel, n_gx, n_gy), out_shape...]
where the time goes in v4:
time: 60 us; the launch traced here: 59.6 us
  Pallas kernels  57.3 us (96%)
  local copies, waits for them, and re-layouts  2.35 us (4%)
    pallas_call x1, Pallas kernels, by_blocks(): pl.pallas_call(functools.partial(butterfly_kernel, n_gx, n_gy), out_shape...  57.3 us
    unnamed x5, local copies, waits for them, and re-layouts  2.35 us

profile of v4, /device:TPU:0, one launch (start us, length us, event | category | flops | bytes accessed | tf_op | source)
XLA Modules:
  0.0 59.6 jit_solution(16945470324277897558)
XLA Ops:
  0.0 0.0 copy-start.1
  0.0 0.7 %copy-done.1 = f32[1,6,64]{2,0,1:T(1,128)S(1)} copy-done((f32[1,6,64]{2,0,1:T(1,128)S(1)}, f32[1,6,64]{2,0,1:T(1,128)}, u32[]{:S(2)}) %copy-start.1) | copy-done | bytes 1560
  0.7 0.0 copy-start
  0.7 0.7 %copy-done = f32[14,64]{1,0:T(8,128)S(1)} copy-done((f32[14,64]{1,0:T(8,128)S(1)}, f32[14,64]{1,0:T(8,128)}, u32[]{:S(2)}) %copy-start) | copy-done | bytes 3608
  1.4 57.3 %butterfly.1 = f32[4,4,4,32,128]{4,3,2,1,0:T(8,128)S(1)} custom-call(f32[16,128,128]{2,1,0:T(8,128)} %bitcast.5, f32[6,1,64]{2,1,0:T(1,128)S(1)} %bitcast.4, f32[14,64]{1,0:T(8,128)S(1)} %copy-done), custom_call_target="tpu_custom_call" | custom-call | tf_op jit(solution)/shard_map/butterfly/pallas_call | solution.py:528
  58.6 1.0 %copy.5 = f32[1,64,32,128]{3,2,1,0:T(8,128)} copy(f32[1,64,32,128]{3,2,1,0:T(8,128)S(1)} %bitcast.3) | data formatting | bytes 2097152
Async XLA Ops:
  0.0 0.7 %copy-start.1 = (f32[1,6,64]{2,0,1:T(1,128)S(1)}, f32[1,6,64]{2,0,1:T(1,128)}, u32[]{:S(2)}) copy-start(f32[1,6,64]{2,0,1:T(1,128)} %param.4) | copy-start | bytes 4612
  0.7 0.7 %copy-start = (f32[14,64]{1,0:T(8,128)S(1)}, f32[14,64]{1,0:T(8,128)}, u32[]{:S(2)}) copy-start(f32[14,64]{1,0:T(8,128)} %cs_ref.1) | copy-start | bytes 10756
